TPU v7x, 32 devices: a whole 2x2x4 slice. The times are simulated.
32 devices in a mesh: dp: 8 (over z, y), tensor: 4 (over x, core).
Axes of the slice: x: 2, y: 2, z: 4, core: 2. Of those that a mesh axis runs over, the one named last changes fastest.
Arguments:
- tokens: bfloat16 [8, 256, 8192], P('dp', 'tensor'), may hold values from -6 to 6
- cotangent: bfloat16 [8, 256, 14336], P('dp', 'tensor'), may hold values from -6 to 6
- weights: bfloat16 [8, 112, 2, 2, 128, 128], P('dp', 'tensor'), may hold values from -6 to 6
- momentum: bfloat16 [8, 112, 2, 2, 128, 128], P('dp', 'tensor'), may hold values from -4 to 4
- pattern: int32 [112, 2], P('tensor'), may hold values from 0 to 63, all different within a row
- step: int32 [], replicated, may hold values from 0 to 4095
Outputs:
- hidden: bfloat16 [8, 256, 14336], P('dp', 'tensor')
- new_weights: bfloat16 [8, 112, 2, 2, 128, 128], P('dp', 'tensor')
- new_momentum: bfloat16 [8, 112, 2, 2, 128, 128], P('dp', 'tensor')
Inputs may be any that keep to these rules, and one draw needn't show every extreme that they name: `pattern`: each row names 2 different input blocks; every input block is named by some row.
All inputs are finite; a program needn't handle non-finite values.
Results may differ from a plain program's by a relative error of at most 0.0058.
Values may be sent and summed in bfloat16 or wider, within the bound.
A program may use at most 128 MiB of HBM per device.

v0:
```python
from functools import partial

import jax
import jax.numpy as jnp
from jax import lax
from jax.experimental import pallas as pl
from jax.experimental.pallas import tpu as pltpu
from jax.sharding import PartitionSpec as P

BLOCK = 128
KB = 2
SCALE = (KB * BLOCK) ** (-0.5)
MESH = pl.DeviceIdType.MESH
FIRST = 10
AHEAD = 4


def stepped_of(packed, moved):
    return (packed.astype(jnp.float32) - 0.1 * moved.astype(jnp.float32)).astype(jnp.bfloat16)


def average(one, other):
    return ((one.astype(jnp.float32) + other.astype(jnp.float32)) * 0.5).astype(jnp.bfloat16)


def kernel(
    distance,
    replicas,
    groups,
    pat_hbm,
    tok_ref,
    cot_ref,
    w_ref,
    m_ref,
    hid_out,
    nw_out,
    nm_out,
    tok_in,
    tok_mine,
    tok_all,
    cot_all,
    hid_all,
    w_own,
    m_own,
    w_far,
    m_far,
    pat_ref,
    in_sem,
    w_sem,
    m_send,
    m_recv,
    tok_send,
    tok_recv,
    cot_send,
    cot_recv,
    hid_send,
    hid_recv,
):
    own_blocks = w_ref.shape[0]
    rows = tok_ref.shape[0]
    input_blocks = tok_ref.shape[1] // BLOCK
    width = own_blocks * BLOCK
    seq = rows * groups
    here = lax.axis_index("tensor")
    replica = lax.axis_index("dp")
    ahead = {"dp": lax.rem(replica + distance, replicas)}
    behind = {"dp": lax.rem(replica + replicas - distance, replicas)}
    peers = [lax.rem(here + o, groups) for o in range(1, groups)]

    barrier = pltpu.get_barrier_semaphore()
    greeted = [{"tensor": q} for q in peers] + [ahead]
    if 2 * distance != replicas:
        greeted.append(behind)
    for device in greeted:
        pl.semaphore_signal(barrier, inc=1, device_id=device, device_id_type=MESH)

    def own_columns(q):
        return pl.ds(pl.multiple_of(q * width, BLOCK), width)

    loads = [
        pltpu.make_async_copy(tok_ref, tok_in, in_sem.at[0]),
        pltpu.make_async_copy(cot_ref.at[:, own_columns(here)], cot_all.at[here], in_sem.at[1]),
        pltpu.make_async_copy(w_ref, w_own, in_sem.at[2]),
        pltpu.make_async_copy(m_ref, m_own, in_sem.at[3]),
        pltpu.make_async_copy(pat_hbm, pat_ref, in_sem.at[4]),
    ]
    for load in loads:
        load.start()
    pl.semaphore_wait(barrier, len(greeted))

    tok_copies = [
        pltpu.make_async_remote_copy(
            src_ref=tok_mine,
            dst_ref=tok_all.at[:, here],
            send_sem=tok_send.at[i],
            recv_sem=tok_recv.at[i],
            device_id={"tensor": q},
            device_id_type=MESH,
        )
        for i, q in enumerate(peers)
    ]
    cot_copies = [
        pltpu.make_async_remote_copy(
            src_ref=cot_ref.at[:, own_columns(q)],
            dst_ref=cot_all.at[here],
            send_sem=cot_send.at[i],
            recv_sem=cot_recv.at[i],
            device_id={"tensor": q},
            device_id_type=MESH,
        )
        for i, q in enumerate(peers)
    ]
    w_copy = pltpu.make_async_remote_copy(
        src_ref=w_ref,
        dst_ref=w_far,
        send_sem=w_sem.at[0],
        recv_sem=w_sem.at[1],
        device_id=ahead,
        device_id_type=MESH,
    )
    w_copy.start()
    loads[0].wait()
    for b in range(input_blocks):
        tok_mine[b] = tok_in[:, b * BLOCK : (b + 1) * BLOCK]
    for copy in tok_copies:
        copy.start()
    for copy in cot_copies:
        copy.start()
    tok_own = pltpu.make_async_copy(tok_mine, tok_all.at[:, here], in_sem.at[0])
    tok_own.start()
    for load in loads[1:] + [tok_own]:
        load.wait()
    for copy in tok_copies + cot_copies:
        copy.wait()

    def moved_copy(j):
        return pltpu.make_async_remote_copy(
            src_ref=m_own.at[j],
            dst_ref=m_far.at[j],
            send_sem=m_send.at[j],
            recv_sem=m_recv.at[j],
            device_id=ahead,
            device_id_type=MESH,
        )

    def make_block(j):
        cols = pl.ds(pl.multiple_of(j * BLOCK, BLOCK), BLOCK)
        chosen = jnp.concatenate(
            [tok_all[pat_ref[k, j]].reshape(seq, BLOCK) for k in range(KB)], axis=1
        )
        packed = jnp.concatenate(
            [w_own[j, u].reshape(KB * BLOCK, BLOCK) for u in range(2)], axis=1
        )
        both = jnp.dot(chosen, packed, preferred_element_type=jnp.float32) * SCALE
        gate, up = both[:, :BLOCK], both[:, BLOCK:]
        sigma = jax.nn.sigmoid(gate)
        gated = gate * sigma
        hid_all[:, :, cols] = (gated * up).astype(jnp.bfloat16).reshape(groups, rows, BLOCK)
        back = cot_all[:, :, cols].reshape(seq, BLOCK).astype(jnp.float32)
        dgate = (back * up * sigma * (1.0 + gate * (1.0 - sigma))).astype(jnp.bfloat16)
        duptail = (back * gated).astype(jnp.bfloat16)
        tails = jnp.concatenate([dgate, duptail], axis=1)
        grad = (
            lax.dot_general(
                chosen, tails, (((0,), (0,)), ((), ())), preferred_element_type=jnp.float32
            )
            * SCALE
        )
        for u in range(2):
            old = m_own[j, u].reshape(KB * BLOCK, BLOCK).astype(jnp.float32)
            new = (0.9 * old + grad[:, u * BLOCK : (u + 1) * BLOCK]).astype(jnp.bfloat16)
            m_own[j, u] = new.reshape(KB, BLOCK, BLOCK)

    burst = min(FIRST, own_blocks)

    def make_and_send(j, carry):
        make_block(j)
        moved_copy(j).start()
        return carry

    def make_only(j, carry):
        make_block(j)
        return carry

    lax.fori_loop(0, burst, make_and_send, 0)
    lax.fori_loop(burst, own_blocks, make_only, 0)

    hid_copies = [
        pltpu.make_async_remote_copy(
            src_ref=hid_all.at[q],
            dst_ref=hid_out.at[:, own_columns(here)],
            send_sem=hid_send.at[i],
            recv_sem=hid_recv.at[i],
            device_id={"tensor": q},
            device_id_type=MESH,
        )
        for i, q in enumerate(peers)
    ]
    for copy in hid_copies:
        copy.start()
    hid_own = pltpu.make_async_copy(
        hid_all.at[here], hid_out.at[:, own_columns(here)], in_sem.at[0]
    )
    hid_own.start()

    w_copy.wait()

    def mix_block(j, carry):
        moved_copy(j).wait_send()
        later = j + AHEAD

        @pl.when(jnp.logical_and(later >= burst, later < own_blocks))
        def _():
            moved_copy(later).start()

        moved_copy(j).wait_recv()
        moved, far_moved = m_own[j], m_far[j]
        nw_out[j] = average(stepped_of(w_own[j], moved), stepped_of(w_far[j], far_moved))
        nm_out[j] = average(moved, far_moved)
        return carry

    lax.fori_loop(0, own_blocks, mix_block, 0)

    for copy in hid_copies:
        copy.wait()
    hid_own.wait()


def write_kernel(hid_ref, nw_ref, nm_ref, hid_out, nw_out, nm_out, sems):
    pairs = ((hid_ref, hid_out), (nw_ref, nw_out), (nm_ref, nm_out))
    copies = []
    for i, (src, dst) in enumerate(pairs):
        half = src.shape[0] // 2
        for k in range(2):
            part = pl.ds(k * half, half)
            copies.append(pltpu.make_async_copy(src.at[part], dst.at[part], sems.at[i, k]))
    for copy in copies:
        copy.start()
    for copy in copies:
        copy.wait()


def written(*results):
    held = [pltpu.with_memory_space_constraint(r, pltpu.VMEM) for r in results]
    return pl.pallas_call(
        write_kernel,
        out_shape=tuple(jax.ShapeDtypeStruct(r.shape, r.dtype) for r in results),
        in_specs=[pl.BlockSpec(memory_space=pltpu.VMEM)] * len(results),
        out_specs=(pl.BlockSpec(memory_space=pltpu.HBM),) * len(results),
        scratch_shapes=[pltpu.SemaphoreType.DMA((len(results), 2))],
        compiler_params=pltpu.CompilerParams(vmem_limit_bytes=1024 * 1024),
    )(*held)


def run(distance, replicas, groups, number, pattern, tokens, cotangent, weights, momentum):
    rows, model = tokens.shape
    own_blocks = weights.shape[0]
    width = own_blocks * BLOCK
    bf16 = jnp.bfloat16
    anywhere = pl.BlockSpec(memory_space=pl.ANY)
    others = groups - 1
    dma = pltpu.SemaphoreType.DMA
    results = pl.pallas_call(
        partial(kernel, distance, replicas, groups),
        out_shape=(
            pltpu.VMEM(cotangent.shape, bf16),
            pltpu.VMEM(weights.shape, bf16),
            pltpu.VMEM(weights.shape, bf16),
        ),
        in_specs=[anywhere] * 5,
        out_specs=(pl.BlockSpec(memory_space=pltpu.VMEM),) * 3,
        scratch_shapes=[
            pltpu.VMEM((rows, model), bf16),
            pltpu.VMEM((model // BLOCK, rows, BLOCK), bf16),
            pltpu.VMEM((model // BLOCK, groups, rows, BLOCK), bf16),
            pltpu.VMEM((groups, rows, width), bf16),
            pltpu.VMEM((groups, rows, width), bf16),
            pltpu.VMEM(weights.shape, bf16),
            pltpu.VMEM(weights.shape, bf16),
            pltpu.VMEM(weights.shape, bf16),
            pltpu.VMEM(weights.shape, bf16),
            pltpu.SMEM(pattern.shape, jnp.int32),
            dma((5,)),
            dma((2,)),
            dma((own_blocks,)),
            dma((own_blocks,)),
            dma((others,)),
            dma((others,)),
            dma((others,)),
            dma((others,)),
            dma((others,)),
            dma((others,)),
        ],
        compiler_params=pltpu.CompilerParams(
            collective_id=number, has_side_effects=True, vmem_limit_bytes=42 * 1024 * 1024
        ),
        cost_estimate=pl.CostEstimate(
            flops=8 * groups * rows * KB * BLOCK * width,
            bytes_accessed=2 * (groups * rows * model + 6 * weights.size),
            transcendentals=groups * rows * width,
        ),
    )(pattern, tokens, cotangent, weights, momentum)
    return written(*results)


def per_device(tokens, cotangent, weights, momentum, pattern, step):
    replicas = lax.axis_size("dp")
    groups = lax.axis_size("tensor")
    levels = replicas.bit_length() - 1
    branches = [partial(run, 2**level, replicas, groups, level) for level in range(levels)]
    hidden, new_weights, new_momentum = lax.switch(
        lax.rem(step, levels), branches, pattern.T, tokens[0], cotangent[0], weights[0], momentum[0]
    )
    return (hidden[None], new_weights[None], new_momentum[None])


def solution(mesh):
    in_specs = (
        P("dp", "tensor", None),
        P("dp", "tensor", None),
        P("dp", "tensor", None, None, None, None),
        P("dp", "tensor", None, None, None, None),
        P("tensor", None),
        P(),
    )
    out_specs = (
        P("dp", "tensor", None),
        P("dp", "tensor", None, None, None, None),
        P("dp", "tensor", None, None, None, None),
    )
    return jax.shard_map(
        per_device, mesh=mesh, in_specs=in_specs, out_specs=out_specs, check_vma=False
    )
```

profile of v0, /device:TPU:0, one launch (start us, length us, event | category | flops | bytes accessed | tf_op | source)
XLA Modules:
  0.0 327.2 jit_solution(7409729911049369045)
XLA Ops:
  1.3 325.9 %conditional.1 = ((bf16[64,14336]{1,0:T(8,128)(2,1)}, bf16[28,2,2,128,128]{4,3,2,1,0:T(8,128)(2,1)}, bf16[28,2,2,128,128]{4,3,2,1,0:T(8,128)(2,1)})) conditional(s32[]{:T(128)} %clamp.3, (bf16[1,64,8192]{2,1,0:T(8,128)(2,1)}, bf16[1,64,14336]{2,1,0:T(8,128)(2,1)}, bf16[1,28,2,2,128,128]{5,4,3,2,1,0:T(8,128)(2,1)}, ...), branch_computations={%region_0.0_spmd.clone, %region_1.0_spmd.clone, %region_2.0_spmd.c... | conditional | flops 1879048192 | bytes 26214408 | solution.py:311
  1.3 322.2 %branch_2_fun.2 = (bf16[64,14336]{1,0:T(8,128)(2,1)S(1)}, bf16[28,2,2,128,128]{4,3,2,1,0:T(8,128)(2,1)S(1)}, bf16[28,2,2,128,128]{4,3,2,1,0:T(8,128)(2,1)S(1)}) custom-call(s32[2,28]{1,0:T(2,128)} %get-tuple-element.113.pat_hbm, bf16[64,8192]{1,0:T(8,128)(2,1)} %bitcast.27, bf16[64,14336]{1,0:T(8,128)(2,1)} %bitcast.24, ...), custom_call_target="tpu_custom_call" | custom-call | flops 1879048192 | bytes 26214400 | tf_op jit(solution)/shard_map/cond/branch_2_fun/pallas_call | solution.py:263
  323.6 3.6 %branch_2_fun.3 = (bf16[64,14336]{1,0:T(8,128)(2,1)}, bf16[28,2,2,128,128]{4,3,2,1,0:T(8,128)(2,1)}, bf16[28,2,2,128,128]{4,3,2,1,0:T(8,128)(2,1)}) custom-call(bf16[64,14336]{1,0:T(8,128)(2,1)S(1)} %get-tuple-element.118.hid_ref, bf16[28,2,2,128,128]{4,3,2,1,0:T(8,128)(2,1)S(1)} %get-tuple-element.119.nw_ref, ...), custom_call_target="tpu_custom_call" | custom-call | tf_op jit(solution)/shard_map/cond/branch_2_fun/pallas_call | solution.py:245
where the time goes:
time: 327 us
  Pallas kernels  326 us (100%)
    pallas_call x1, Pallas kernels, run(): pl.pallas_call(partial(kernel, distance, replicas, groups), out_shape=(pl...  322 us

commit v1 on v0

--- a/solution.py
+++ b/solution.py
@@ -68,9 +68,9 @@
     peers = [lax.rem(here + o, groups) for o in range(1, groups)]
 
     barrier = pltpu.get_barrier_semaphore()
-    greeted = [{"tensor": q} for q in peers] + [ahead]
+    greeted = [behind] + [{"tensor": q} for q in peers]
     if 2 * distance != replicas:
-        greeted.append(behind)
+        greeted.append(ahead)
     for device in greeted:
         pl.semaphore_signal(barrier, inc=1, device_id=device, device_id_type=MESH)
 
@@ -226,13 +226,19 @@
     hid_own.wait()
 
 
+def pieces_of(array):
+    unit = 16 if len(array.shape) == 2 else 1
+    return max(k for k in (1, 2, 4) if array.shape[0] % (k * unit) == 0)
+
+
 def write_kernel(hid_ref, nw_ref, nm_ref, hid_out, nw_out, nm_out, sems):
     pairs = ((hid_ref, hid_out), (nw_ref, nw_out), (nm_ref, nm_out))
     copies = []
     for i, (src, dst) in enumerate(pairs):
-        half = src.shape[0] // 2
-        for k in range(2):
-            part = pl.ds(k * half, half)
+        pieces = pieces_of(src)
+        size = src.shape[0] // pieces
+        for k in range(pieces):
+            part = pl.ds(k * size, size)
             copies.append(pltpu.make_async_copy(src.at[part], dst.at[part], sems.at[i, k]))
     for copy in copies:
         copy.start()
@@ -247,7 +253,7 @@
         out_shape=tuple(jax.ShapeDtypeStruct(r.shape, r.dtype) for r in results),
         in_specs=[pl.BlockSpec(memory_space=pltpu.VMEM)] * len(results),
         out_specs=(pl.BlockSpec(memory_space=pltpu.HBM),) * len(results),
-        scratch_shapes=[pltpu.SemaphoreType.DMA((len(results), 2))],
+        scratch_shapes=[pltpu.SemaphoreType.DMA((len(results), 4))],
         compiler_params=pltpu.CompilerParams(vmem_limit_bytes=1024 * 1024),
     )(*held)
 

time: 327 us -> 172 us (0.53)
  Pallas kernels: 326 us -> 171 us
    pallas_call x1, Pallas kernels: 322 us -> 167 us  [run(): pl.pallas_call(partial(kernel, distance, replicas, groups), out_shape=(pl...]
where the time goes in v1:
time: 172 us
  Pallas kernels  171 us (99%)
    pallas_call x1, Pallas kernels, run(): pl.pallas_call(partial(kernel, distance, replicas, groups), out_shape=(pl...  167 us
    pallas_call x1, Pallas kernels, written(): pl.pallas_call(write_kernel, out_shape=tuple((jax.ShapeDtypeStruct(r.shap...  3.64 us

profile of v1, /device:TPU:0, one launch (start us, length us, event | category | flops | bytes accessed | tf_op | source)
XLA Modules:
  0.0 171.9 jit_solution(8292858518167755099)
XLA Ops:
  1.3 170.6 %conditional.1 = ((bf16[64,14336]{1,0:T(8,128)(2,1)}, bf16[28,2,2,128,128]{4,3,2,1,0:T(8,128)(2,1)}, bf16[28,2,2,128,128]{4,3,2,1,0:T(8,128)(2,1)})) conditional(s32[]{:T(128)} %clamp.3, (bf16[1,64,8192]{2,1,0:T(8,128)(2,1)}, bf16[1,64,14336]{2,1,0:T(8,128)(2,1)}, bf16[1,28,2,2,128,128]{5,4,3,2,1,0:T(8,128)(2,1)}, ...), branch_computations={%region_0.0_spmd.clone, %region_1.0_spmd.clone, %region_2.0_spmd.c... | conditional | flops 1879048192 | bytes 26214408 | solution.py:317
  1.3 166.9 %branch_0_fun.2 = (bf16[64,14336]{1,0:T(8,128)(2,1)S(1)}, bf16[28,2,2,128,128]{4,3,2,1,0:T(8,128)(2,1)S(1)}, bf16[28,2,2,128,128]{4,3,2,1,0:T(8,128)(2,1)S(1)}) custom-call(s32[2,28]{1,0:T(2,128)} %get-tuple-element.95.pat_hbm, bf16[64,8192]{1,0:T(8,128)(2,1)} %bitcast.25, bf16[64,14336]{1,0:T(8,128)(2,1)} %bitcast.22, ...), custom_call_target="tpu_custom_call" | custom-call | flops 1879048192 | bytes 26214400 | tf_op jit(solution)/shard_map/cond/branch_0_fun/pallas_call | solution.py:269
  168.2 3.6 %branch_0_fun.3 = (bf16[64,14336]{1,0:T(8,128)(2,1)}, bf16[28,2,2,128,128]{4,3,2,1,0:T(8,128)(2,1)}, bf16[28,2,2,128,128]{4,3,2,1,0:T(8,128)(2,1)}) custom-call(bf16[64,14336]{1,0:T(8,128)(2,1)S(1)} %get-tuple-element.100.hid_ref, bf16[28,2,2,128,128]{4,3,2,1,0:T(8,128)(2,1)S(1)} %get-tuple-element.101.nw_ref, ...), custom_call_target="tpu_custom_call" | custom-call | tf_op jit(solution)/shard_map/cond/branch_0_fun/pallas_call | solution.py:251
